TPU v7x, 128 devices: a whole 4x4x4 slice. The times are simulated.
128 devices in a mesh: dp: 32 (over y, z, core), tensor: 4 (over x).
Axes of the slice: x: 4, y: 4, z: 4, core: 2. Of those that a mesh axis runs over, the one named last changes fastest.
Arguments:
- tokens: bfloat16 [32768, 768], P('dp'), may hold values from -6 to 6
- lengths: int32 [32, 8], P('dp'), may hold values from 1 to 512, 1024 in all within a row
- attn_gain: float32 [768], replicated, may hold values from 0.1 to 1.9
- query_weight: bfloat16 [768, 768], P(None, 'tensor'), may hold values from -0.21875 to 0.21875
- key_weight: bfloat16 [768, 768], P(None, 'tensor'), may hold values from -0.21875 to 0.21875
- value_weight: bfloat16 [768, 768], P(None, 'tensor'), may hold values from -0.21875 to 0.21875
- output_weight: bfloat16 [768, 768], P('tensor'), may hold values from -0.875 to 0.875
- ffn_gain: float32 [768], replicated, may hold values from 0.1 to 1.9
- gate_weight: bfloat16 [768, 2048], P(None, 'tensor'), may hold values from -0.21875 to 0.21875
- up_weight: bfloat16 [768, 2048], P(None, 'tensor'), may hold values from -0.21875 to 0.21875
- down_weight: bfloat16 [2048, 768], P('tensor'), may hold values from -0.125 to 0.125
- cotangent: bfloat16 [32768, 768], P('dp'), may hold values from -6 to 6
Outputs:
- layer_out: bfloat16 [32768, 768], P('dp')
- token_grad: float32 [32768, 768], P('dp')
- attn_gain_grad: float32 [768], replicated
- query_grad: float32 [768, 768], P(None, 'tensor')
- key_grad: float32 [768, 768], P(None, 'tensor')
- value_grad: float32 [768, 768], P(None, 'tensor')
- output_grad: float32 [768, 768], P('tensor')
- ffn_gain_grad: float32 [768], replicated
- gate_grad: float32 [768, 2048], P(None, 'tensor')
- up_grad: float32 [768, 2048], P(None, 'tensor')
- down_grad: float32 [2048, 768], P('tensor')
Inputs may be any that keep to these rules, and one draw needn't show every extreme that they name: Each row's 8 lengths add up to 1024; the longest segment of every row has exactly 512 blocks.
All inputs are finite; a program needn't handle non-finite values.
Results may differ from a plain program's by a relative error of at most 0.015.
Values sent between devices are 32-bit elements; how exact they have to be, the bound alone decides.
No kernel may reach another device: no remote copies, remote signals or barrier semaphores. Data moves between devices by JAX's collectives and lax.ppermute only.
A program may use at most 128 MiB of HBM per device.

v0:
```python
import jax
import jax.numpy as jnp
from jax import lax
from jax.sharding import PartitionSpec as P

HEAD = 64


epsilon = 1e-06


def norm_forward(values):
    factor = lax.rsqrt(jnp.mean(values * values, axis=-1, keepdims=True) + epsilon)
    return (values * factor, factor)


def norm_backward(grad, based, factor, gain):
    scaled = grad * gain
    inner = jnp.mean(scaled * based, axis=-1, keepdims=True)
    return (factor * (scaled - based * inner), jnp.sum(grad * based, axis=0))


def gelu_product(gate, upper):
    return jax.nn.gelu(gate, approximate=True) * upper


def mat(left, right):
    return jnp.dot(left, right, preferred_element_type=jnp.float32)


def local(
    tokens,
    lengths,
    attn_gain,
    query_weight,
    key_weight,
    value_weight,
    output_weight,
    ffn_gain,
    gate_weight,
    up_weight,
    down_weight,
    cotangent,
):
    rows = tokens.shape[0]
    width = query_weight.shape[1]
    heads_here = width // HEAD
    factor_head = HEAD ** (-0.5)
    ends = jnp.cumsum(lengths[0])
    places = jnp.arange(rows, dtype=jnp.int32)
    ids = jnp.sum((places[:, None] >= ends[None, :-1]).astype(jnp.int32), axis=1)
    same = (ids[:, None] == ids[None, :])[None]
    inputs = tokens.astype(jnp.float32)
    based_one, factor_one = norm_forward(inputs)
    normed_one = (based_one * attn_gain).astype(jnp.bfloat16)
    query = mat(normed_one, query_weight).astype(jnp.bfloat16)
    keys = mat(normed_one, key_weight).astype(jnp.bfloat16)
    values = mat(normed_one, value_weight).astype(jnp.bfloat16)
    query_heads = query.reshape(rows, heads_here, HEAD)
    key_heads = keys.reshape(rows, heads_here, HEAD)
    value_heads = values.reshape(rows, heads_here, HEAD)
    scores = (
        jnp.einsum("qhd,khd->hqk", query_heads, key_heads, preferred_element_type=jnp.float32)
        * factor_head
    )
    scores = jnp.where(same, scores, jnp.float32(-1e30))
    top = jnp.max(scores, axis=-1, keepdims=True)
    expo = jnp.exp(scores - top)
    total = jnp.sum(expo, axis=-1, keepdims=True)
    logsum = top + jnp.log(total)
    probs_low = (expo / total).astype(jnp.bfloat16)
    mixed = jnp.einsum("hqk,khd->qhd", probs_low, value_heads, preferred_element_type=jnp.float32)
    mixed = mixed.astype(jnp.bfloat16).reshape(rows, width)
    attn = lax.psum(mat(mixed, output_weight), "tensor")
    middle = inputs + attn
    based_two, factor_two = norm_forward(middle)
    normed_two = (based_two * ffn_gain).astype(jnp.bfloat16)
    gate = mat(normed_two, gate_weight)
    upper = mat(normed_two, up_weight)
    product, product_pull = jax.vjp(gelu_product, gate, upper)
    hidden = product.astype(jnp.bfloat16)
    ffn = lax.psum(mat(hidden, down_weight), "tensor")
    layer_out = (middle + ffn).astype(jnp.bfloat16)
    grad_out = cotangent.astype(jnp.float32)
    down_grad = mat(hidden.T, cotangent)
    grad_hidden = mat(cotangent, down_weight.T)
    grad_gate, grad_upper = product_pull(grad_hidden)
    grad_gate = grad_gate.astype(jnp.bfloat16)
    grad_upper = grad_upper.astype(jnp.bfloat16)
    gate_grad = mat(normed_two.T, grad_gate)
    up_grad = mat(normed_two.T, grad_upper)
    grad_normed_two = lax.psum(
        mat(grad_gate, gate_weight.T) + mat(grad_upper, up_weight.T), "tensor"
    )
    grad_from_two, ffn_gain_grad = norm_backward(grad_normed_two, based_two, factor_two, ffn_gain)
    grad_middle = grad_out + grad_from_two
    grad_attn = grad_middle.astype(jnp.bfloat16)
    output_grad = mat(mixed.T, grad_attn)
    grad_mixed = (
        mat(grad_attn, output_weight.T).astype(jnp.bfloat16).reshape(rows, heads_here, HEAD)
    )
    again = (
        jnp.einsum("qhd,khd->hqk", query_heads, key_heads, preferred_element_type=jnp.float32)
        * factor_head
    )
    probs = jnp.where(same, jnp.exp(again - logsum), jnp.float32(0.0))
    probs_again = probs.astype(jnp.bfloat16)
    grad_values = jnp.einsum(
        "hqk,qhd->khd", probs_again, grad_mixed, preferred_element_type=jnp.float32
    )
    grad_values = grad_values.astype(jnp.bfloat16).reshape(rows, width)
    grad_probs = jnp.einsum(
        "qhd,khd->hqk", grad_mixed, value_heads, preferred_element_type=jnp.float32
    )
    grad_scores = probs * (grad_probs - jnp.sum(grad_probs * probs, axis=-1, keepdims=True))
    grad_scores = grad_scores.astype(jnp.bfloat16)
    grad_query = (
        jnp.einsum("hqk,khd->qhd", grad_scores, key_heads, preferred_element_type=jnp.float32)
        * factor_head
    )
    grad_query = grad_query.astype(jnp.bfloat16).reshape(rows, width)
    grad_keys = (
        jnp.einsum("hqk,qhd->khd", grad_scores, query_heads, preferred_element_type=jnp.float32)
        * factor_head
    )
    grad_keys = grad_keys.astype(jnp.bfloat16).reshape(rows, width)
    query_grad = mat(normed_one.T, grad_query)
    key_grad = mat(normed_one.T, grad_keys)
    value_grad = mat(normed_one.T, grad_values)
    partial_one = (
        mat(grad_query, query_weight.T)
        + mat(grad_keys, key_weight.T)
        + mat(grad_values, value_weight.T)
    )
    grad_normed_one = lax.psum(partial_one, "tensor")
    grad_from_one, attn_gain_grad = norm_backward(grad_normed_one, based_one, factor_one, attn_gain)
    token_grad = grad_middle + grad_from_one
    (
        attn_gain_grad,
        query_grad,
        key_grad,
        value_grad,
        output_grad,
        ffn_gain_grad,
        gate_grad,
        up_grad,
        down_grad,
    ) = lax.psum(
        (
            attn_gain_grad,
            query_grad,
            key_grad,
            value_grad,
            output_grad,
            ffn_gain_grad,
            gate_grad,
            up_grad,
            down_grad,
        ),
        "dp",
    )
    return (
        layer_out,
        token_grad,
        attn_gain_grad,
        query_grad,
        key_grad,
        value_grad,
        output_grad,
        ffn_gain_grad,
        gate_grad,
        up_grad,
        down_grad,
    )


def solution(mesh):
    placed = (
        P("dp", None),
        P("dp", None),
        P(),
        P(None, "tensor"),
        P(None, "tensor"),
        P(None, "tensor"),
        P("tensor", None),
        P(),
        P(None, "tensor"),
        P(None, "tensor"),
        P("tensor", None),
        P("dp", None),
    )
    return jax.shard_map(
        local,
        mesh=mesh,
        in_specs=placed,
        out_specs=(
            P("dp", None),
            P("dp", None),
            P(),
            P(None, "tensor"),
            P(None, "tensor"),
            P(None, "tensor"),
            P("tensor", None),
            P(),
            P(None, "tensor"),
            P(None, "tensor"),
            P("tensor", None),
        ),
        check_vma=False,
    )
```

profile of v0, /device:TPU:1, one launch (start us, length us, event | category | flops | bytes accessed | tf_op | source)
XLA Modules:
  0.0 515.5 jit_solution(17283885867437373472)
XLA Ops:
  7.3 1.9 fusion.16
  9.2 1.8 fusion.10
  11.0 1.4 convolution_convert_fusion.2
  12.4 1.4 convolution_convert_fusion.1
  14.8 1.6 convolution_convert_fusion.3
  16.5 5.9 %select_reduce_fusion = (f32[3,1024]{1,0:T(4,128)S(1)}, f32[3,1024,1024]{1,2,0:T(8,128)}) fusion(pred[1024,1024]{0,1:T(8,128)(4,1)S(1)} %broadcast_compare_fusion, bf16[1024,3,64]{0,2,1:T(8,128)(2,1)S(1)} %bitcast.83, bf16[1024,3,64]{0,2,1:T(8,128)(2,1)S(1)} %bitcast.81), kind=kOutput, calls=%fused_computation.5 | convolution fusion | flops 412087296 | bytes 14430208 | tf_op jit(solution)/shard_map/qhd,khd->hqk/dot_general | solution.py:63
  22.4 7.3 %fusion = f32[3,1024]{1,0:T(4,128)S(1)} fusion(f32[3,1024,1024]{1,2,0:T(8,128)} %get-tuple-element.32, f32[3,1024]{1,0:T(4,128)S(1)} %get-tuple-element.31, pred[1024,1024]{0,1:T(8,128)(4,1)S(1)} %broadcast_compare_fusion), kind=kLoop, calls=%fused_computation.6 | loop fusion | flops 12579840 | bytes 13656064 | tf_op jit(solution)/shard_map/reduce_sum | solution.py:69
  29.7 6.8 %fusion.29 = bf16[3,64,1024]{2,1,0:T(8,128)(2,1)S(1)} fusion(bf16[1024,3,64]{0,2,1:T(8,128)(2,1)S(1)} %bitcast.85, f32[3,1024,1024]{1,2,0:T(8,128)} %get-tuple-element.32, f32[3,1024]{1,0:T(4,128)S(1)} %fusion, f32[3,1024]{1,0:T(4,128)S(1)} %get-tuple-element.31, pred[1024,1024]{0,1:T(8,128)(4,1)S(1)} %broadcast_compare_fusion), kind=kOutput, calls=%fused_computation.55 | convolution fusion | flops 418578432 | bytes 14442496 | tf_op jit(solution)/shard_map/hqk,khd->qhd/dot_general | solution.py:72
  37.4 2.3 fusion.37
  39.9 78.8 %all-reduce.8.cloned.1.call-done = f32[1024,768]{1,0:T(8,128)} async-done(((f32[1024,768]{1,0:T(8,128)}), f32[1024,768]{1,0:T(8,128)}) %all-reduce.8.cloned.1.call-update) | async-done | bytes 3145744 | tf_op jit(solution)/shard_map/psum | solution.py:74
  118.7 2.4 multiply_reduce_fusion.3
  121.5 1.3 copy-done.32
  122.8 1.0 fusion.38
  124.5 1.0 fusion.39
  125.9 3.3 multiply_convert_fusion.2
  129.2 1.0 copy-done.28
  130.1 1.0 fusion.41
  131.2 2.7 convolution_add_fusion
  134.0 3.8 fusion.40
  137.8 71.8 %all-reduce.10.cloned.1.call-done = f32[1024,768]{1,0:T(8,128)} async-done(((f32[1024,768]{1,0:T(8,128)}), f32[1024,768]{1,0:T(8,128)}) %all-reduce.10.cloned.1.call-update) | async-done | bytes 3145744 | tf_op jit(solution)/shard_map/psum | solution.py:92
  209.6 3.8 multiply_reduce_fusion.1
  214.3 2.4 multiply_add_fusion
  216.8 1.7 copy-done.4
  219.1 6.5 %fusion.24 = bf16[3,64,1024]{2,1,0:T(8,128)(2,1)S(1)} fusion(bf16[1024,3,64]{0,2,1:T(8,128)(2,1)S(1)} %bitcast.75, f32[3,1024,1024]{1,2,0:T(8,128)} %get-tuple-element.32, f32[3,1024]{1,0:T(4,128)S(1)} %log_add_fusion, pred[1024,1024]{0,1:T(8,128)(4,1)S(1)} %broadcast_compare_fusion), kind=kOutput, calls=%fused_computation.48 | convolution fusion | flops 415432704 | bytes 14430208 | tf_op jit(solution)/shard_map/hqk,qhd->khd/dot_general | solution.py:108
  225.7 6.7 %multiply_reduce_fusion = (f32[3,1024]{1,0:T(4,128)S(1)}, f32[3,1024,1024]{1,2,0:T(8,128)}) fusion(f32[3,1024,1024]{1,2,0:T(8,128)S(1)} %bitcast.70, f32[3,1024]{1,0:T(4,128)S(1)} %log_add_fusion, pred[1024,1024]{0,1:T(8,128)(4,1)S(1)} %broadcast_compare_fusion, bf16[1024,3,64]{0,2,1:T(8,128)(2,1)S(1)} %bitcast.76, bf16[1024,3,64]{0,2,1:T(8,128)(2,1)S(1)} %bitcast.86), kind=kOutput, calls=%fused_computation.1 | convolution fusion | flops 418378752 | bytes 27025408 | tf_op jit(solution)/shard_map/qhd,khd->hqk/dot_general | solution.py:112
  232.4 7.0 %multiply_convert_fusion = bf16[3,1024,1024]{1,2,0:T(8,128)(2,1)S(1)} fusion(f32[3,1024,1024]{1,2,0:T(8,128)} %get-tuple-element.34, f32[3,1024,1024]{1,2,0:T(8,128)S(1)} %bitcast.70, f32[3,1024]{1,0:T(4,128)S(1)} %get-tuple-element.33, f32[3,1024]{1,0:T(4,128)S(1)} %log_add_fusion, pred[1024,1024]{0,1:T(8,128)(4,1)S(1)} %broadcast_compare_fusion), kind=kLoop, calls=%fused_computation | loop fusion | flops 18874368 | bytes 32530432 | tf_op jit(solution)/shard_map/convert_element_type | solution.py:116
  239.5 2.0 fusion.28
  241.5 1.2 fusion.27
  244.3 2.4 add_add_fusion
  247.0 0.9 copy-done.29
  247.9 3.7 fusion.44
  251.7 2.1 fusion.45
  253.8 2.2 fusion.46
  256.0 1.3 fusion.49
  257.3 1.3 fusion.48
  258.6 1.3 fusion.47
  259.9 1.3 fusion.30
  261.2 112.5 %all-reduce.14.cloned.1.call-done = (f32[1024,768]{1,0:T(8,128)}, f32[1024,768]{1,0:T(8,128)}) async-done(((f32[1024,768]{1,0:T(8,128)}, f32[1024,768]{1,0:T(8,128)}), (f32[1024,768]{1,0:T(8,128)}, f32[1024,768]{1,0:T(8,128)})) %all-reduce.14.cloned.1.call-update) | async-done | bytes 6291472 | tf_op jit(solution)/shard_map/psum | solution.py:82
  373.7 2.8 fusion.15
  376.5 65.2 %all-reduce = (f32[768]{0:T(1024)}, f32[768]{0:T(1024)}) all-reduce(f32[768]{0:T(1024)S(1)} %get-tuple-element.13, f32[768]{0:T(1024)S(1)} %get-tuple-element.11), channel_id=1, replica_groups=mesh['dp'=32,'tensor'=4] {'dp'}, use_global_device_ids=true, to_apply=%region_14.15 | all-reduce | flops 1536 | bytes 12288 | tf_op jit(solution)/shard_map/psum | solution.py:148
  441.7 7.4 %fusion.14 = (f32[1024,768]{1,0:T(8,128)}, bf16[1024,768]{1,0:T(8,128)(2,1)}) fusion(f32[1024,768]{1,0:T(8,128)} %copy-done.4, bf16[1024,768]{1,0:T(8,128)(2,1)S(1)} %copy-done.6, f32[1024,768]{1,0:T(8,128)} %get-tuple-element.25, f32[1024]{0:T(1024)S(1)} %broadcast_multiply_fusion, f32[768]{0:T(1024)S(1)} %copy-done.43, f32[1024]{0:T(1024)S(1)} %add_rsqrt_fusion.1, ...), kind=kLoop, calls=%fused_computation.22 | loop fusion | flops 7077888 | bytes 18885632 | tf_op jit(solution)/shard_map/add | solution.py:137
  449.2 49.5 %all-reduce.12.cloned.1.call-done = (f32[768,192]{0,1:T(8,128)}, f32[768,192]{0,1:T(8,128)}, f32[768,192]{0,1:T(8,128)}, f32[192,768]{1,0:T(8,128)}, f32[768,512...) async-done(((f32[768,192]{0,1:T(8,128)}, f32[768,192]{0,1:T(8,128)}, f32[768,192]{0,1:T(8,128)}, f32[192,768]{1,0:T(8,128)}, f32[768,512]{1,0:T(8,128)}, ...) | async-done | bytes 7077904 | tf_op jit(solution)/shard_map/psum | solution.py:148
  498.6 2.1 copy.46
  500.7 2.0 copy.47
  502.7 1.9 copy.48
  505.5 1.1 copy.50
  506.6 1.1 copy.51
  507.8 1.1 copy.52
  (115 shorter events, 7.9 us)
Async XLA Ops:
  7.2 118.3 %copy-start = (bf16[512,768]{1,0:T(8,128)(2,1)S(1)}, bf16[512,768]{1,0:T(8,128)(2,1)}, u32[]{:S(2)}) copy-start(bf16[512,768]{1,0:T(8,128)(2,1)} %param.22) | copy-start | bytes 2359300
  7.2 3.8 copy-start.40
  7.2 5.2 %copy-start.38 = (bf16[768,192]{0,1:T(8,128)(2,1)S(1)}, bf16[768,192]{0,1:T(8,128)(2,1)}, u32[]{:S(2)}) copy-start(bf16[768,192]{0,1:T(8,128)(2,1)} %param.16) | copy-start | bytes 884740
  7.2 111.5 %all-reduce.8.cloned.1.call-start = ((), (), s32[]{:S(2)}) async-start(), calls=%async_computation | async-start | bytes 6291456 | tf_op jit(solution)/shard_map/psum | solution.py:74
  9.2 4.7 copy-start.44
  11.0 5.4 %copy-start.7 = (bf16[1024,768]{1,0:T(8,128)(2,1)}, bf16[1024,768]{1,0:T(8,128)(2,1)S(1)}, u32[]{:S(2)}) copy-start(bf16[1024,768]{1,0:T(8,128)(2,1)S(1)} %fusion.10) | copy-start | bytes 4718596
  14.0 2.4 copy-start.22
  14.0 2.4 copy-start.24
  16.4 13.3 %copy-start.34 = (bf16[1024,192]{0,1:T(8,128)(2,1)}, bf16[1024,192]{0,1:T(8,128)(2,1)S(1)}, u32[]{:S(2)}) copy-start(bf16[1024,192]{0,1:T(8,128)(2,1)S(1)} %convolution_convert_fusion.3) | copy-start | bytes 1179652
  29.7 7.6 %copy-start.26 = (bf16[192,768]{1,0:T(8,128)(2,1)S(1)}, bf16[192,768]{1,0:T(8,128)(2,1)}, u32[]{:S(2)}) copy-start(bf16[192,768]{1,0:T(8,128)(2,1)} %param.18) | copy-start | bytes 884740
  37.4 81.4 %copy-start.6 = (bf16[1024,768]{1,0:T(8,128)(2,1)S(1)}, bf16[1024,768]{1,0:T(8,128)(2,1)}, u32[]{:S(2)}) copy-start(bf16[1024,768]{1,0:T(8,128)(2,1)} %param.12) | copy-start | bytes 4718596
  39.7 81.5 %copy-start.42 = (f32[768]{0:T(1024)S(1)}, f32[768]{0:T(1024)}, u32[]{:S(2)}) copy-start(f32[768]{0:T(1024)} %param.19) | copy-start | bytes 9220
  39.7 169.9 %all-reduce.10.cloned.1.call-start = ((), (), s32[]{:S(2)}) async-start(), calls=%async_computation.1 | async-start | bytes 6291456 | tf_op jit(solution)/shard_map/psum | solution.py:92
  121.1 2.7 copy-start.2
  121.1 1.7 copy-start.32
  122.8 1.7 copy-start.33
  124.5 1.4 copy-start.18
  129.2 2.0 copy-start.30
  133.9 239.8 %all-reduce.14.cloned.1.call-start = ((), (), s32[]{:S(2)}) async-start(), calls=%async_computation.3 | async-start | bytes 12582912 | tf_op jit(solution)/shard_map/psum | solution.py:82
  209.6 3.8 copy-start.3
  209.6 4.7 copy-start.9
  214.3 4.1 copy-start.27
  214.3 11.3 %slice-start = ((s8[12582912]{0:T(1024)(128)(4,1)}), s8[4194304]{0:T(1024)(128)(4,1)S(1)}, s32[]{:S(2)}) async-start(s8[12582912]{0:T(1024)(128)(4,1)} %bitcast.69), calls=%async_computation.4 | async-start | bytes 8388608
  216.8 1.7 copy-start.4
  218.4 7.2 %slice-start.1 = ((s8[12582912]{0:T(1024)(128)(4,1)}), s8[4194304]{0:T(1024)(128)(4,1)S(1)}, s32[]{:S(2)}) async-start(s8[12582912]{0:T(1024)(128)(4,1)} %bitcast.69), calls=%async_computation.5 | async-start | bytes 8388608
  219.1 6.6 %slice-start.2 = ((s8[12582912]{0:T(1024)(128)(4,1)}), s8[4194304]{0:T(1024)(128)(4,1)S(1)}, s32[]{:S(2)}) async-start(s8[12582912]{0:T(1024)(128)(4,1)} %bitcast.69), calls=%async_computation.6 | async-start | bytes 8388608
  219.1 6.6 %copy-start.35 = (bf16[1024,192]{0,1:T(8,128)(2,1)S(1)}, bf16[1024,192]{0,1:T(8,128)(2,1)}, u32[]{:S(2)}) copy-start(bf16[1024,192]{0,1:T(8,128)(2,1)} %copy-done.34) | copy-start | bytes 1179652
  225.7 18.6 %copy-start.11 = (bf16[3,64,1024]{2,1,0:T(8,128)(2,1)}, bf16[3,64,1024]{2,1,0:T(8,128)(2,1)S(1)}, u32[]{:S(2)}) copy-start(bf16[3,64,1024]{2,1,0:T(8,128)(2,1)S(1)} %fusion.24) | copy-start | bytes 1179652
  232.4 7.0 %copy-start.25 = (bf16[1024,192]{0,1:T(8,128)(2,1)S(1)}, bf16[1024,192]{0,1:T(8,128)(2,1)}, u32[]{:S(2)}) copy-start(bf16[1024,192]{0,1:T(8,128)(2,1)} %convolution_convert_fusion.2) | copy-start | bytes 1179652
  239.4 2.1 copy-start.23
  241.5 1.2 copy-start.39
  242.8 1.6 copy-start.37
  246.7 1.2 copy-start.29
  246.7 251.9 %all-reduce.12.cloned.1.call-start = ((), (), s32[]{:S(2)}) async-start(), calls=%async_computation.2 | async-start | bytes 14155776 | tf_op jit(solution)/shard_map/psum | solution.py:148
  247.9 3.7 copy-start.17
  247.9 3.7 copy-start.31
  251.7 2.2 copy-start.10
  251.7 2.2 copy-start.19
  253.8 2.2 copy-start.8
  253.8 2.2 copy-start.12
  257.3 2.6 copy-start.5
  257.3 2.6 copy-start.21
  261.2 112.5 %copy-start.43 = (f32[768]{0:T(1024)S(1)}, f32[768]{0:T(1024)}, u32[]{:S(2)}) copy-start(f32[768]{0:T(1024)} %param.14) | copy-start | bytes 9220
  498.6 6.0 %copy-start.36 = (f32[192,768]{1,0:T(8,128)S(1)}, f32[192,768]{1,0:T(8,128)}, u32[]{:S(2)}) copy-start(f32[192,768]{1,0:T(8,128)} %get-tuple-element.43) | copy-start | bytes 1769476
  498.6 6.8 %copy-start.15 = (f32[768,512]{1,0:T(8,128)S(1)}, f32[768,512]{1,0:T(8,128)}, u32[]{:S(2)}) copy-start(f32[768,512]{1,0:T(8,128)} %get-tuple-element.45) | copy-start | bytes 4718596
  500.7 5.9 %copy-start.14 = (f32[768,512]{1,0:T(8,128)S(1)}, f32[768,512]{1,0:T(8,128)}, u32[]{:S(2)}) copy-start(f32[768,512]{1,0:T(8,128)} %get-tuple-element.46) | copy-start | bytes 4718596
  505.5 2.3 copy-start.13
  505.5 3.4 copy-start.1
  (4 other events, 3.8 us)
Sparse Core Ops, SparseCore 0:
  39.8 78.8 all-reduce.7
  134.0 75.5 all-reduce.9
  246.9 126.8 all-reduce.13
  379.2 119.4 all-reduce.11
where the time goes:
time: 516 us; the launch traced here: 515 us
  waiting for transfers between devices  313 us (61%)
  matrix products  66.3 us (13%)
  blocking collectives  65.2 us (13%)
  other arithmetic  38.1 us (7%)
  local copies, waits for them, and re-layouts  18.4 us (4%)
  between operations  14.3 us (3%)
    psum x1, waiting for transfers between devices, local(): ffn = lax.psum(mat(hidden, down_weight), 'tensor')  112 us
    psum x1, waiting for transfers between devices, local(): attn = lax.psum(mat(mixed, output_weight), 'tensor')  78.8 us
    psum x1, waiting for transfers between devices, local(): lax.psum(mat(grad_gate, gate_weight.T) + mat(grad_upper, up_weight.T), 't...  71.8 us
    psum x1, blocking collectives, local(): lax.psum((attn_gain_grad, query_grad, key_grad, value_grad, output_grad,...  65.2 us
    psum x1, waiting for transfers between devices, local(): lax.psum((attn_gain_grad, query_grad, key_grad, value_grad, output_grad,...  49.5 us
    dot_general x21, matrix products, mat(): return jnp.dot(left, right, preferred_element_type=jnp.float32)  37 us
    unnamed x103, local copies, waits for them, and re-layouts  18.4 us
  transfers between devices with their start and end apart: 4, of which 4 were waited for; matrix products, arithmetic and copies ran while one was open for 5% of the time, Pallas kernels for 0%

commit v1 on v0

--- a/solution.py
+++ b/solution.py
@@ -79,7 +79,10 @@
     upper = mat(normed_two, up_weight)
     product, product_pull = jax.vjp(gelu_product, gate, upper)
     hidden = product.astype(jnp.bfloat16)
-    ffn = lax.psum(mat(hidden, down_weight), "tensor")
+    ffn_part = mat(hidden, down_weight)
+    ffn = ffn_part
+    for shift in (1, 3, 2):
+        ffn = ffn + lax.ppermute(ffn_part, "tensor", [(i, (i + shift) % 4) for i in range(4)])
     layer_out = (middle + ffn).astype(jnp.bfloat16)
     grad_out = cotangent.astype(jnp.float32)
     down_grad = mat(hidden.T, cotangent)

time: 516 us -> 579 us (1.12)
  waiting for transfers between devices: 313 us -> 376 us
  matrix products: 66.3 us -> 60.5 us
    psum x1, waiting for transfers between devices: 71.8 us -> 184 us  [local(): lax.psum(mat(grad_gate, gate_weight.T) + mat(grad_upper, up_weight.T), 't...]
    psum x1, waiting for transfers between devices: 112 us -> 61 us  [local(): grad_normed_one = lax.psum(partial_one, 'tensor')]
    add x1, other arithmetic: 2.44 us -> 8.52 us  [local(): grad_middle = grad_out + grad_from_two]
    unnamed x103 -> x101, local copies, waits for them, and re-layouts: 18.4 us -> 17.6 us
  transfers between devices with their start and end apart: 4 -> 7, of which waited for: 4 -> 4; matrix products, arithmetic and copies ran while one was open for 5% -> 5% of each run, Pallas kernels for 0% -> 0%
where the time goes in v1:
time: 579 us
  waiting for transfers between devices  376 us (65%)
  blocking collectives  65.4 us (11%)
  matrix products  60.5 us (10%)
  other arithmetic  42 us (7%)
  local copies, waits for them, and re-layouts  17.6 us (3%)
  between operations  14.3 us (2%)
    psum x1, waiting for transfers between devices, local(): lax.psum(mat(grad_gate, gate_weight.T) + mat(grad_upper, up_weight.T), 't...  184 us
    psum x1, waiting for transfers between devices, local(): attn = lax.psum(mat(mixed, output_weight), 'tensor')  78.8 us
    psum x1, blocking collectives, local(): lax.psum((attn_gain_grad, query_grad, key_grad, value_grad, output_grad,...  65.4 us
    psum x1, waiting for transfers between devices, local(): grad_normed_one = lax.psum(partial_one, 'tensor')  61 us
    psum x1, waiting for transfers between devices, local(): lax.psum((attn_gain_grad, query_grad, key_grad, value_grad, output_grad,...  51.2 us
    dot_general x21, matrix products, mat(): return jnp.dot(left, right, preferred_element_type=jnp.float32)  34.7 us
    unnamed x101, local copies, waits for them, and re-layouts  17.6 us
  transfers between devices with their start and end apart: 7, of which 4 were waited for; matrix products, arithmetic and copies ran while one was open for 5% of the time, Pallas kernels for 0%

profile of v1, /device:TPU:1, one launch (start us, length us, event | category | flops | bytes accessed | tf_op | source)
XLA Modules:
  0.0 578.7 jit_solution(5411898244406414291)
XLA Ops:
  7.2 1.9 fusion.16
  9.2 0.8 reduce-window.4
  10.8 1.2 fusion.10
  14.1 5.9 %select_reduce_fusion = (f32[3,1024]{1,0:T(4,128)S(1)}, f32[3,1024,1024]{1,2,0:T(8,128)}) fusion(pred[1024,1024]{0,1:T(8,128)(4,1)S(1)} %broadcast_compare_fusion, bf16[1024,3,64]{0,2,1:T(8,128)(2,1)S(1)} %bitcast.81, bf16[1024,3,64]{0,2,1:T(8,128)(2,1)S(1)} %bitcast.83), kind=kOutput, calls=%fused_computation.5 | convolution fusion | flops 412087296 | bytes 14430208 | tf_op jit(solution)/shard_map/qhd,khd->hqk/dot_general | solution.py:63
  20.0 7.3 %fusion = f32[3,1024]{1,0:T(4,128)S(1)} fusion(f32[3,1024,1024]{1,2,0:T(8,128)} %get-tuple-element.32, f32[3,1024]{1,0:T(4,128)S(1)} %get-tuple-element.31, pred[1024,1024]{0,1:T(8,128)(4,1)S(1)} %broadcast_compare_fusion), kind=kLoop, calls=%fused_computation.6 | loop fusion | flops 12579840 | bytes 13656064 | tf_op jit(solution)/shard_map/reduce_sum | solution.py:69
  27.4 6.8 %fusion.29 = bf16[3,64,1024]{2,1,0:T(8,128)(2,1)S(1)} fusion(bf16[1024,3,64]{0,2,1:T(8,128)(2,1)S(1)} %bitcast.85, f32[3,1024,1024]{1,2,0:T(8,128)} %get-tuple-element.32, f32[3,1024]{1,0:T(4,128)S(1)} %fusion, f32[3,1024]{1,0:T(4,128)S(1)} %get-tuple-element.31, pred[1024,1024]{0,1:T(8,128)(4,1)S(1)} %broadcast_compare_fusion), kind=kOutput, calls=%fused_computation.55 | convolution fusion | flops 418578432 | bytes 14442496 | tf_op jit(solution)/shard_map/hqk,khd->qhd/dot_general | solution.py:72
  35.0 2.3 fusion.37
  37.5 78.8 %all-reduce.7.cloned.1.call-done = f32[1024,768]{1,0:T(8,128)} async-done(((f32[1024,768]{1,0:T(8,128)}), f32[1024,768]{1,0:T(8,128)}) %all-reduce.7.cloned.1.call-update) | async-done | bytes 3145744 | tf_op jit(solution)/shard_map/psum | solution.py:74
  116.3 2.4 multiply_reduce_fusion.3
  119.1 1.3 copy-done.31
  120.4 1.0 fusion.38
  122.1 1.0 fusion.39
  123.5 3.3 multiply_convert_fusion.2
  126.8 1.0 copy-done.27
  127.8 1.0 fusion.41
  128.8 2.7 convolution_add_fusion
  131.6 3.9 fusion.40
  135.5 1.3 collective-permute-start.2
  136.8 1.2 collective-permute-start.1
  138.3 184.4 %all-reduce.9.cloned.1.call-done = f32[1024,768]{1,0:T(8,128)} async-done(((f32[1024,768]{1,0:T(8,128)}), f32[1024,768]{1,0:T(8,128)}) %all-reduce.9.cloned.1.call-update) | async-done | bytes 3145744 | tf_op jit(solution)/shard_map/psum | solution.py:95
  322.7 3.8 multiply_reduce_fusion.1
  326.6 8.5 %multiply_add_fusion = (f32[1024,768]{1,0:T(8,128)S(1)}, bf16[1024,768]{1,0:T(8,128)(2,1)}) fusion(bf16[1024,768]{1,0:T(8,128)(2,1)S(1)} %copy-done.12, f32[1024,768]{1,0:T(8,128)} %all-reduce.9.cloned.1.call-done, f32[1024,768]{1,0:T(8,128)} %copy-done.2, f32[1024]{0:T(1024)S(1)} %broadcast_multiply_fusion.1, f32[768]{0:T(1024)S(1)} %copy-done.42, ...), kind=kLoop, calls=%fused_computation.27 | loop fusion | flops 9437184 | bytes 25177088 | tf_op jit(solution)/shard_map/add | solution.py:99
  335.2 1.7 copy-done.3
  337.5 6.7 %multiply_reduce_fusion = (f32[3,1024]{1,0:T(4,128)S(1)}, f32[3,1024,1024]{1,2,0:T(8,128)}) fusion(f32[3,1024,1024]{1,2,0:T(8,128)S(1)} %bitcast.70, f32[3,1024]{1,0:T(4,128)S(1)} %log_add_fusion, pred[1024,1024]{0,1:T(8,128)(4,1)S(1)} %broadcast_compare_fusion, bf16[1024,3,64]{0,2,1:T(8,128)(2,1)S(1)} %bitcast.75, bf16[1024,3,64]{0,2,1:T(8,128)(2,1)S(1)} %bitcast.86), kind=kOutput, calls=%fused_computation.1 | convolution fusion | flops 418378752 | bytes 27025408 | tf_op jit(solution)/shard_map/qhd,khd->hqk/dot_general | solution.py:115
  344.3 7.0 %multiply_convert_fusion = bf16[3,1024,1024]{1,2,0:T(8,128)(2,1)S(1)} fusion(f32[3,1024,1024]{1,2,0:T(8,128)} %get-tuple-element.34, f32[3,1024,1024]{1,2,0:T(8,128)S(1)} %bitcast.70, f32[3,1024]{1,0:T(4,128)S(1)} %get-tuple-element.33, f32[3,1024]{1,0:T(4,128)S(1)} %log_add_fusion, pred[1024,1024]{0,1:T(8,128)(4,1)S(1)} %broadcast_compare_fusion), kind=kLoop, calls=%fused_computation | loop fusion | flops 18874368 | bytes 32530432 | tf_op jit(solution)/shard_map/convert_element_type | solution.py:119
  351.3 1.2 fusion.27
  352.5 2.0 fusion.28
  354.6 3.0 fusion.24
  359.4 2.3 add_add_fusion
  362.0 0.9 copy-done.28
  362.9 3.7 fusion.44
  366.7 2.1 fusion.45
  368.8 2.2 fusion.46
  371.0 1.3 fusion.47
  372.3 1.3 fusion.48
  373.6 1.3 fusion.49
  374.9 1.3 fusion.30
  376.2 61.0 %all-reduce.11.cloned.1.call-done = f32[1024,768]{1,0:T(8,128)} async-done(((f32[1024,768]{1,0:T(8,128)}), f32[1024,768]{1,0:T(8,128)}) %all-reduce.11.cloned.1.call-update) | async-done | bytes 3145744 | tf_op jit(solution)/shard_map/psum | solution.py:138
  437.3 2.8 fusion.15
  440.0 65.4 %all-reduce = (f32[768]{0:T(1024)}, f32[768]{0:T(1024)}) all-reduce(f32[768]{0:T(1024)S(1)} %get-tuple-element.13, f32[768]{0:T(1024)S(1)} %get-tuple-element.11), channel_id=1, replica_groups=mesh['dp'=32,'tensor'=4] {'dp'}, use_global_device_ids=true, to_apply=%region_13.14 | all-reduce | flops 1536 | bytes 12288 | tf_op jit(solution)/shard_map/psum | solution.py:151
  505.4 5.3 fusion.14
  510.7 51.2 %all-reduce.13.cloned.1.call-done = (f32[768,192]{0,1:T(8,128)}, f32[768,192]{0,1:T(8,128)}, f32[768,192]{0,1:T(8,128)}, f32[192,768]{1,0:T(8,128)}, f32[768,512...) async-done(((f32[768,192]{0,1:T(8,128)}, f32[768,192]{0,1:T(8,128)}, f32[768,192]{0,1:T(8,128)}, f32[192,768]{1,0:T(8,128)}, f32[768,512]{1,0:T(8,128)}, ...) | async-done | bytes 7077904 | tf_op jit(solution)/shard_map/psum | solution.py:151
  561.9 2.1 copy.45
  564.0 2.0 copy.46
  566.0 1.9 copy.47
  568.7 1.1 copy.49
  569.9 1.1 copy.50
  571.0 1.1 copy.51
  (119 shorter events, 9.3 us)
Async XLA Ops:
  7.2 115.9 %copy-start = (bf16[512,768]{1,0:T(8,128)(2,1)S(1)}, bf16[512,768]{1,0:T(8,128)(2,1)}, u32[]{:S(2)}) copy-start(bf16[512,768]{1,0:T(8,128)(2,1)} %param.22) | copy-start | bytes 2359300
  7.2 3.6 copy-start.5
  7.2 109.1 %all-reduce.7.cloned.1.call-start = ((), (), s32[]{:S(2)}) async-start(), calls=%async_computation | async-start | bytes 6291456 | tf_op jit(solution)/shard_map/psum | solution.py:74
  10.0 1.9 copy-start.36
  10.1 2.6 copy-start.38
  10.8 2.6 copy-start.40
  12.0 2.1 copy-start.6
  12.7 14.7 %copy-start.33 = (bf16[1024,192]{0,1:T(8,128)(2,1)}, bf16[1024,192]{0,1:T(8,128)(2,1)S(1)}, u32[]{:S(2)}) copy-start(bf16[1024,192]{0,1:T(8,128)(2,1)S(1)} %convolution_convert_fusion.3) | copy-start | bytes 1179652
  13.4 6.6 %copy-start.21 = (bf16[1024,192]{0,1:T(8,128)(2,1)}, bf16[1024,192]{0,1:T(8,128)(2,1)S(1)}, u32[]{:S(2)}) copy-start(bf16[1024,192]{0,1:T(8,128)(2,1)S(1)} %convolution_convert_fusion.2) | copy-start | bytes 1179652
  14.1 6.0 %copy-start.23 = (bf16[1024,192]{0,1:T(8,128)(2,1)}, bf16[1024,192]{0,1:T(8,128)(2,1)S(1)}, u32[]{:S(2)}) copy-start(bf16[1024,192]{0,1:T(8,128)(2,1)S(1)} %convolution_convert_fusion.1) | copy-start | bytes 1179652
  27.4 7.6 %copy-start.25 = (bf16[192,768]{1,0:T(8,128)(2,1)S(1)}, bf16[192,768]{1,0:T(8,128)(2,1)}, u32[]{:S(2)}) copy-start(bf16[192,768]{1,0:T(8,128)(2,1)} %param.18) | copy-start | bytes 884740
  37.3 81.5 %copy-start.42 = (f32[768]{0:T(1024)S(1)}, f32[768]{0:T(1024)}, u32[]{:S(2)}) copy-start(f32[768]{0:T(1024)} %param.19) | copy-start | bytes 9220
  37.3 285.4 %all-reduce.9.cloned.1.call-start = ((), (), s32[]{:S(2)}) async-start(), calls=%async_computation.1 | async-start | bytes 6291456 | tf_op jit(solution)/shard_map/psum | solution.py:95
  118.7 2.7 copy-start.2
  118.7 1.7 copy-start.31
  120.4 1.7 copy-start.32
  122.1 1.4 copy-start.11
  126.8 2.0 copy-start.29
  131.6 305.7 %all-reduce.11.cloned.1.call-start = ((), (), s32[]{:S(2)}) async-start(), calls=%async_computation.2 | async-start | bytes 6291456 | tf_op jit(solution)/shard_map/psum | solution.py:138
  135.5 191.1 %collective-permute-start.2 = (f32[1024,768]{1,0:T(8,128)}, f32[1024,768]{1,0:T(8,128)}, u32[]{:S(2)}, u32[]{:S(2)}) collective-permute-start(f32[1024,768]{1,0:T(8,128)} %fusion.40), channel_id=1, source_target_pairs={{0,2},{1,3},{2,0},{3,1},{4,6},{5,7},{6,4},{7,5},{8,10},{9,11},{10,... | collective-permute-start | bytes 9437192 | tf_op jit(solution)/shard_map/ppermute | solution.py:85
  136.8 189.8 %collective-permute-start.1 = (f32[1024,768]{1,0:T(8,128)}, f32[1024,768]{1,0:T(8,128)}, u32[]{:S(2)}, u32[]{:S(2)}) collective-permute-start(f32[1024,768]{1,0:T(8,128)} %fusion.40), channel_id=1, source_target_pairs={{0,3},{1,0},{2,1},{3,2},{4,7},{5,4},{6,5},{7,6},{8,11},{9,8},{10,9... | collective-permute-start | bytes 9437192 | tf_op jit(solution)/shard_map/ppermute | solution.py:85
  138.0 188.6 %collective-permute-start = (f32[1024,768]{1,0:T(8,128)}, f32[1024,768]{1,0:T(8,128)}, u32[]{:S(2)}, u32[]{:S(2)}) collective-permute-start(f32[1024,768]{1,0:T(8,128)} %fusion.40), channel_id=1, source_target_pairs={{0,1},{1,2},{2,3},{3,0},{4,5},{5,6},{6,7},{7,4},{8,9},{9,10},{10,1... | collective-permute-start | bytes 9437192 | tf_op jit(solution)/shard_map/ppermute | solution.py:85
  322.7 3.9 copy-start.12
  322.7 14.8 %slice-start = ((s8[12582912]{0:T(1024)(128)(4,1)}), s8[4194304]{0:T(1024)(128)(4,1)S(1)}, s32[]{:S(2)}) async-start(s8[12582912]{0:T(1024)(128)(4,1)} %bitcast.69), calls=%async_computation.4 | async-start | bytes 8388608
  326.6 10.3 %copy-start.26 = (bf16[192,768]{1,0:T(8,128)(2,1)S(1)}, bf16[192,768]{1,0:T(8,128)(2,1)}, u32[]{:S(2)}) copy-start(bf16[192,768]{1,0:T(8,128)(2,1)} %param.18) | copy-start | bytes 884740
  326.6 10.9 %slice-start.1 = ((s8[12582912]{0:T(1024)(128)(4,1)}), s8[4194304]{0:T(1024)(128)(4,1)S(1)}, s32[]{:S(2)}) async-start(s8[12582912]{0:T(1024)(128)(4,1)} %bitcast.69), calls=%async_computation.5 | async-start | bytes 8388608
  326.6 10.9 %slice-start.2 = ((s8[12582912]{0:T(1024)(128)(4,1)}), s8[4194304]{0:T(1024)(128)(4,1)S(1)}, s32[]{:S(2)}) async-start(s8[12582912]{0:T(1024)(128)(4,1)} %bitcast.69), calls=%async_computation.6 | async-start | bytes 8388608
  335.2 1.7 copy-start.3
  335.2 2.4 copy-start.34
  344.3 7.0 %copy-start.24 = (bf16[1024,192]{0,1:T(8,128)(2,1)S(1)}, bf16[1024,192]{0,1:T(8,128)(2,1)}, u32[]{:S(2)}) copy-start(bf16[1024,192]{0,1:T(8,128)(2,1)} %copy-done.23) | copy-start | bytes 1179652
  354.6 3.1 copy-start.39
  357.6 1.7 copy-start.9
  357.7 1.7 copy-start.37
  361.7 200.2 %all-reduce.13.cloned.1.call-start = ((), (), s32[]{:S(2)}) async-start(), calls=%async_computation.3 | async-start | bytes 14155776 | tf_op jit(solution)/shard_map/psum | solution.py:151
  362.9 3.7 copy-start.18
  362.9 3.7 copy-start.30
  366.6 2.2 copy-start.8
  366.6 2.2 copy-start.13
  368.8 2.2 copy-start.7
  371.0 2.6 copy-start.10
  372.3 2.6 copy-start.4
  372.3 2.6 copy-start.20
  376.2 61.0 %copy-start.43 = (f32[768]{0:T(1024)S(1)}, f32[768]{0:T(1024)}, u32[]{:S(2)}) copy-start(f32[768]{0:T(1024)} %param.14) | copy-start | bytes 9220
  561.9 6.0 %copy-start.35 = (f32[192,768]{1,0:T(8,128)S(1)}, f32[192,768]{1,0:T(8,128)}, u32[]{:S(2)}) copy-start(f32[192,768]{1,0:T(8,128)} %get-tuple-element.41) | copy-start | bytes 1769476
  561.9 6.8 %copy-start.16 = (f32[768,512]{1,0:T(8,128)S(1)}, f32[768,512]{1,0:T(8,128)}, u32[]{:S(2)}) copy-start(f32[768,512]{1,0:T(8,128)} %get-tuple-element.43) | copy-start | bytes 4718596
  564.0 5.9 %copy-start.15 = (f32[768,512]{1,0:T(8,128)S(1)}, f32[768,512]{1,0:T(8,128)}, u32[]{:S(2)}) copy-start(f32[768,512]{1,0:T(8,128)} %get-tuple-element.44) | copy-start | bytes 4718596
  568.7 2.3 copy-start.14
  568.7 3.4 copy-start.1
  (6 other events, 6.4 us)
Sparse Core Ops, SparseCore 0:
  37.4 78.8 all-reduce.6
  131.7 191.0 all-reduce.8
  361.9 75.3 all-reduce.10
  442.7 119.1 all-reduce.12
